TPU v7x, 32 devices: a whole 2x2x4 slice. The times are simulated.
32 devices in a mesh: sect: 2 (over x), blk: 16 (over z, y, core).
Axes of the slice: x: 2, y: 2, z: 4, core: 2. Of those that a mesh axis runs over, the one named last changes fastest.
Arguments:
- bits: int32 [2, 256], P('sect', 'blk'), may hold values from 0 to 1
- labels: int32 [128], replicated, may hold values from 0 to 127, each once
- left: bfloat16 [256, 16384], P('blk')
- tensors: bfloat16 [2, 2, 128, 128, 128], P('sect', None, 'blk')
Outputs:
- prob: float32 [2, 256], P('sect', 'blk')
- logprob: float32 [2, 256], P('sect', 'blk')
Inputs may be any that keep to these rules, and one draw needn't show every extreme that they name: Every charge labels exactly one block.
All inputs are finite; a program needn't handle non-finite values.
Results may differ from a plain program's by a relative error of at most 0.0003.
Values may be sent and summed in bfloat16 or wider, within the bound.
A program may use at most 64 MiB of HBM per device.

v0:
```python
import jax
import jax.numpy as jnp
from jax import lax
from jax.sharding import PartitionSpec as P


def passed_along(value, axis, steps):
    count = lax.axis_size(axis)
    first, last = (max(0, -steps), min(count, count - steps))
    return lax.ppermute(value, axis, [(source, source + steps) for source in range(first, last)])


def charge_order(labels, left, block):
    count_blocks = labels.shape[0]
    samples_here = left.shape[0]
    blocks = left.reshape(samples_here, count_blocks, block)
    index = jnp.arange(count_blocks, dtype=jnp.int32)
    pick = (labels[None, :] == index[:, None]).astype(jnp.bfloat16)
    ordered = jnp.einsum("ci,rik->rck", pick, blocks, preferred_element_type=jnp.float32)
    return ordered.astype(jnp.bfloat16)


def site_images(state, weights, block):
    count_rows = state.shape[0]
    blocks = state.reshape(count_rows, weights.shape[1], block)
    return jnp.einsum(
        "rck,bckl->brcl",
        blocks,
        weights,
        preferred_element_type=jnp.float32,
        precision=lax.Precision.HIGHEST,
    )


def run_sections(start_rows, site_bits, advance, count):
    segment = lax.axis_index("sect")
    segments = lax.axis_size("sect")
    mrows = start_rows.shape[1]

    def one_step(step, carry):
        state, total, prob_out, log_out = carry
        group = step - segment
        valid = (group >= 0) & (group < count)
        slot = jnp.clip(group, 0, count - 1)
        first = segment == 0
        start_now = lax.dynamic_index_in_dim(start_rows, slot, 0, keepdims=False)
        state = jnp.where(first, start_now, state)
        total = jnp.where(first, jnp.zeros_like(total), total)
        bit_rows = lax.dynamic_index_in_dim(site_bits, slot, 0, keepdims=False)
        prob, next_state = advance(state, bit_rows)
        total = total + jnp.log(prob)
        old_prob = lax.dynamic_index_in_dim(prob_out, slot, 0, keepdims=False)
        old_log = lax.dynamic_index_in_dim(log_out, slot, 0, keepdims=False)
        prob_out = lax.dynamic_update_index_in_dim(
            prob_out, jnp.where(valid, prob, old_prob), slot, 0
        )
        log_out = lax.dynamic_update_index_in_dim(
            log_out, jnp.where(valid, total, old_log), slot, 0
        )
        state, total = passed_along((next_state, total), "sect", 1)
        return (state, total, prob_out, log_out)

    empty = jnp.zeros((count, mrows), jnp.float32)
    init = (start_rows[0], jnp.zeros((mrows,), jnp.float32), empty, empty)
    result = lax.fori_loop(0, count + segments - 1, one_step, init)
    return (result[2], result[3])


def body(bits, labels, left, tensors):
    block = tensors.shape[-1]
    count_blocks = labels.shape[0]
    width = count_blocks * block
    rows = bits.shape[1]
    ordered = charge_order(labels, left, block)
    count = 1
    whole = lax.all_gather(tensors, "blk", axis=2, tiled=True)[0]

    def advance(state, bit_rows):
        image = site_images(state, whole, block)
        stay = image[0]
        raised = jnp.roll(image[1], 1, axis=1)
        norm_zero = jnp.sum(stay * stay, axis=(1, 2))
        norm_one = jnp.sum(raised * raised, axis=(1, 2))
        choose = bit_rows == 1
        chosen_norm = jnp.where(choose, norm_one, norm_zero)
        prob = chosen_norm / (norm_zero + norm_one)
        chosen = jnp.where(choose[:, None, None], raised, stay)
        scaled = chosen * lax.rsqrt(chosen_norm / width + 1e-06)[:, None, None]
        return (prob, scaled.reshape(state.shape[0], width))

    mrows = rows // count
    start_rows = ordered.astype(jnp.float32).reshape(count, mrows, width)
    site_bits = bits[0].reshape(count, mrows)
    prob_out, log_out = run_sections(start_rows, site_bits, advance, count)
    return (prob_out, log_out)


def solution(mesh):
    in_specs = (P("sect", "blk"), P(), P("blk", None), P("sect", None, "blk", None, None))
    out_specs = (P("sect", "blk"), P("sect", "blk"))
    return jax.shard_map(body, mesh=mesh, in_specs=in_specs, out_specs=out_specs, check_vma=False)
```

profile of v0, /device:TPU:0, one launch (start us, length us, event | category | flops | bytes accessed | tf_op | source)
XLA Modules:
  0.0 167.4 jit_solution(3635065234813884847)
XLA Ops:
  7.2 1.9 %copy.15 = bf16[1,2,8,128,128]{4,3,1,0,2:T(8,128)(2,1)} copy(bf16[1,2,8,128,128]{4,3,2,1,0:T(8,128)(2,1)} %param.9) | data formatting | bytes 1048576 | tf_op args[3]
  9.1 1.1 copy.22
  10.3 0.9 fusion.7
  11.2 0.6 copy.29
  11.9 1.2 reshape.91
  13.1 74.7 %all-gather.2.cloned.1.call-done = bf16[1,2,128,128,128]{4,3,1,0,2:T(8,128)(2,1)} async-done(((bf16[1,2,8,128,128]{4,3,1,0,2:T(8,128)(2,1)}), bf16[1,2,128,128,128]{4,3,1,0,2:T(8,128)(2,1)}) %all-gather.2.cloned.1.call-update) | async-done | bytes 8388624 | tf_op jit(solution)/shard_map/all_gather | solution.py:76
  87.8 72.2 %while.21 = (s32[]{:T(128)}, f32[16,16384]{1,0:T(8,128)S(1)}, f32[16]{0:T(128)S(1)}, f32[1,16]{1,0:T(1,128)S(1)}, f32[1,16]{1,0:T(1,128)S(1)}, /*index=5*/s32[1,...) while((s32[]{:T(128)}, f32[16,16384]{1,0:T(8,128)S(1)}, ...), condition=%wide.region_3.4_spmd.clone, body=%wide.region_0.3_spmd.clone.sunk | while | flops 807403776 | bytes 34604624 | solution.py:65
  87.8 1.3 fusion.21
  89.4 6.5 %convolution_bitcast_fusion.2 = f32[2,16,128,128]{3,1,0,2:T(8,128)S(1)} fusion(bf16[2,128,128,128]{3,2,0,1:T(8,128)(2,1)} %get-tuple-element.370, f32[16,128,128,1]{2,1,0,3:T(8,128)S(1)} %bitcast.81), kind=kOutput, calls=%fused_computation.clone.1 | convolution fusion | flops 805306368 | bytes 11534336 | tf_op jit(solution)/shard_map/while/body/eval_jaxpr/rck,bckl->brcl/dot_general | solution.py:26
  95.8 0.4 multiply_reduce_fusion.4
  96.3 0.3 copy.39
  96.9 0.6 fusion.23
  97.6 3.4 %collective-permute-start = (f32[16,16384]{1,0:T(8,128)S(1)}, f32[16,16384]{1,0:T(8,128)S(1)}, u32[]{:S(2)}, u32[]{:S(2)}) collective-permute-start(f32[16,16384]{1,0:T(8,128)S(1)} %fusion.23), channel_id=1, source_target_pairs={{0,16},{1,17},{2,18},{3,19},{4,20},{5,21},{6,22},{7,23},{8,24},{9,... | collective-permute-start | bytes 3145736 | tf_op jit(solution)/shard_map/while/body/eval_jaxpr/ppermute | solution.py:10
  101.0 1.3 collective-permute-start.1
  102.3 21.5 %collective-permute-done.1 = f32[16]{0:T(128)S(1)} collective-permute-done((f32[16]{0:T(128)S(1)}, f32[16]{0:T(128)S(1)}, u32[]{:S(2)}, u32[]{:S(2)}) %collective-permute-start.1) | collective-permute-done | bytes 96 | tf_op jit(solution)/shard_map/while/body/eval_jaxpr/ppermute | solution.py:10
  123.8 1.3 fusion.21
  125.4 6.5 %convolution_bitcast_fusion.2 = f32[2,16,128,128]{3,1,0,2:T(8,128)S(1)} fusion(bf16[2,128,128,128]{3,2,0,1:T(8,128)(2,1)} %get-tuple-element.370, f32[16,128,128,1]{2,1,0,3:T(8,128)S(1)} %bitcast.81), kind=kOutput, calls=%fused_computation.clone.1 | convolution fusion | flops 805306368 | bytes 11534336 | tf_op jit(solution)/shard_map/while/body/eval_jaxpr/rck,bckl->brcl/dot_general | solution.py:26
  131.8 0.4 multiply_reduce_fusion.4
  132.3 0.3 copy.39
  133.0 0.6 fusion.23
  133.6 4.5 %collective-permute-start = (f32[16,16384]{1,0:T(8,128)S(1)}, f32[16,16384]{1,0:T(8,128)S(1)}, u32[]{:S(2)}, u32[]{:S(2)}) collective-permute-start(f32[16,16384]{1,0:T(8,128)S(1)} %fusion.23), channel_id=1, source_target_pairs={{0,16},{1,17},{2,18},{3,19},{4,20},{5,21},{6,22},{7,23},{8,24},{9,... | collective-permute-start | bytes 3145736 | tf_op jit(solution)/shard_map/while/body/eval_jaxpr/ppermute | solution.py:10
  138.1 1.3 collective-permute-start.1
  139.4 20.6 %collective-permute-done.1 = f32[16]{0:T(128)S(1)} collective-permute-done((f32[16]{0:T(128)S(1)}, f32[16]{0:T(128)S(1)}, u32[]{:S(2)}, u32[]{:S(2)}) %collective-permute-start.1) | collective-permute-done | bytes 96 | tf_op jit(solution)/shard_map/while/body/eval_jaxpr/ppermute | solution.py:10
  160.0 0.5 copy-done.1
  (26 shorter events, 1.3 us)
Async XLA Ops:
  7.2 80.6 %copy-start = (s32[1,16]{1,0:T(1,128)S(1)}, s32[1,16]{1,0:T(1,128)}, u32[]{:S(2)}) copy-start(s32[1,16]{1,0:T(1,128)} %param.6) | copy-start | bytes 196
  7.2 80.6 %all-gather.2.cloned.1.call-start = ((), (), s32[]{:S(2)}) async-start(), calls=%async_computation | async-start | bytes 8912896 | tf_op jit(solution)/shard_map/all_gather | solution.py:76
  97.6 26.3 %collective-permute-start = (f32[16,16384]{1,0:T(8,128)S(1)}, f32[16,16384]{1,0:T(8,128)S(1)}, u32[]{:S(2)}, u32[]{:S(2)}) collective-permute-start(f32[16,16384]{1,0:T(8,128)S(1)} %fusion.23), channel_id=1, source_target_pairs={{0,16},{1,17},{2,18},{3,19},{4,20},{5,21},{6,22},{7,23},{8,24},{9,... | collective-permute-start | bytes 3145736 | tf_op jit(solution)/shard_map/while/body/eval_jaxpr/ppermute | solution.py:10
  101.0 22.8 %collective-permute-start.1 = (f32[16]{0:T(128)S(1)}, f32[16]{0:T(128)S(1)}, u32[]{:S(2)}, u32[]{:S(2)}) collective-permute-start(f32[16]{0:T(128)S(1)} %get-tuple-element.336), channel_id=1, source_target_pairs={{0,16},{1,17},{2,18},{3,19},{4,20},{5,21},{6,22},{7,23},{8,24},{9,... | collective-permute-start | bytes 200 | tf_op jit(solution)/shard_map/while/body/eval_jaxpr/ppermute | solution.py:10
  133.6 26.4 %collective-permute-start = (f32[16,16384]{1,0:T(8,128)S(1)}, f32[16,16384]{1,0:T(8,128)S(1)}, u32[]{:S(2)}, u32[]{:S(2)}) collective-permute-start(f32[16,16384]{1,0:T(8,128)S(1)} %fusion.23), channel_id=1, source_target_pairs={{0,16},{1,17},{2,18},{3,19},{4,20},{5,21},{6,22},{7,23},{8,24},{9,... | collective-permute-start | bytes 3145736 | tf_op jit(solution)/shard_map/while/body/eval_jaxpr/ppermute | solution.py:10
  138.1 21.9 %collective-permute-start.1 = (f32[16]{0:T(128)S(1)}, f32[16]{0:T(128)S(1)}, u32[]{:S(2)}, u32[]{:S(2)}) collective-permute-start(f32[16]{0:T(128)S(1)} %get-tuple-element.336), channel_id=1, source_target_pairs={{0,16},{1,17},{2,18},{3,19},{4,20},{5,21},{6,22},{7,23},{8,24},{9,... | collective-permute-start | bytes 200 | tf_op jit(solution)/shard_map/while/body/eval_jaxpr/ppermute | solution.py:10
  160.0 0.5 copy-start.1
  160.0 0.5 copy-start.2
Sparse Core Ops, SparseCore 0:
  10.2 77.5 all-gather.1
where the time goes:
time: 168 us; the launch traced here: 167 us
  waiting for transfers between devices  117 us (70%)
  between operations  14.1 us (8%)
  matrix products  13.9 us (8%)
  starting transfers between devices  10.5 us (6%)
  local copies, waits for them, and re-layouts  6.62 us (4%)
  other arithmetic  5.3 us (3%)
    all_gather x1, waiting for transfers between devices, body(): whole = lax.all_gather(tensors, 'blk', axis=2, tiled=True)[0]  74.7 us
    ppermute x4, waiting for transfers between devices, passed_along(): lax.ppermute(value, axis, [(source, source + steps) for source in range(f...  42.1 us
    dot_general x2, matrix products, site_images(): jnp.einsum('rck,bckl->brcl', blocks, weights, preferred_element_type=jnp....  12.9 us
    ppermute x4, starting transfers between devices, passed_along(): lax.ppermute(value, axis, [(source, source + steps) for source in range(f...  10.5 us
    unnamed x9, local copies, waits for them, and re-layouts  4.15 us
  transfers between devices with their start and end apart: 5, of which 3 were waited for; matrix products, arithmetic and copies ran while one was open for 2% of the time, Pallas kernels for 0%

commit v1 on v0

--- a/solution.py
+++ b/solution.py
@@ -1,7 +1,14 @@
+import functools
+
 import jax
 import jax.numpy as jnp
 from jax import lax
+from jax.experimental import pallas as pl
+from jax.experimental.pallas import tpu as pltpu
 from jax.sharding import PartitionSpec as P
+
+MESH = pl.DeviceIdType.MESH
+EPS = 1e-06
 
 
 def passed_along(value, axis, steps):
@@ -66,13 +73,12 @@
     return (result[2], result[3])
 
 
-def body(bits, labels, left, tensors):
+def body_many(bits, labels, left, tensors):
     block = tensors.shape[-1]
     count_blocks = labels.shape[0]
     width = count_blocks * block
     rows = bits.shape[1]
     ordered = charge_order(labels, left, block)
-    count = 1
     whole = lax.all_gather(tensors, "blk", axis=2, tiled=True)[0]
 
     def advance(state, bit_rows):
@@ -85,17 +91,330 @@
         chosen_norm = jnp.where(choose, norm_one, norm_zero)
         prob = chosen_norm / (norm_zero + norm_one)
         chosen = jnp.where(choose[:, None, None], raised, stay)
-        scaled = chosen * lax.rsqrt(chosen_norm / width + 1e-06)[:, None, None]
+        scaled = chosen * lax.rsqrt(chosen_norm / width + EPS)[:, None, None]
         return (prob, scaled.reshape(state.shape[0], width))
 
-    mrows = rows // count
-    start_rows = ordered.astype(jnp.float32).reshape(count, mrows, width)
-    site_bits = bits[0].reshape(count, mrows)
-    prob_out, log_out = run_sections(start_rows, site_bits, advance, count)
-    return (prob_out, log_out)
+    start_rows = ordered.astype(jnp.float32).reshape(1, rows, width)
+    return run_sections(start_rows, bits[0].reshape(1, rows), advance, 1)
+
+
+def pair_kernel(
+    ranks,
+    bits_ref,
+    labels_ref,
+    left_ref,
+    tens_ref,
+    prob_ref,
+    log_ref,
+    bits_i,
+    labels_v,
+    left_v,
+    left_b,
+    inv_v,
+    inv_s,
+    ordered,
+    state,
+    t0,
+    t1,
+    part,
+    inbox,
+    stack,
+    bits_v,
+    local_sem,
+    tsend_sem,
+    trecv_sem,
+    left_sem,
+    part_sem,
+):
+    sect = lax.axis_index("sect")
+    blk = lax.axis_index("blk")
+    me = sect * ranks + blk
+    total = 2 * ranks
+    rows = bits_ref.shape[1]
+    block = tens_ref.shape[-1]
+    group = tens_ref.shape[2]
+    half = group // 2
+    count_blocks = group * ranks
+    samples = rows * ranks
+    width = count_blocks * block
+    part_width = half * block
+
+    labels_copy = pltpu.make_async_copy(labels_ref, labels_v, local_sem.at[3])
+    labels_copy.start()
+    bits_copy = pltpu.make_async_copy(bits_ref, bits_i, local_sem.at[4])
+    bits_copy.start()
+    left_copy = pltpu.make_async_copy(left_ref, left_v, local_sem.at[0])
+    left_copy.start()
+
+    @pl.when(sect == 0)
+    def _():
+        pltpu.make_async_copy(tens_ref.at[0, :, pl.ds(0, half)], t0, local_sem.at[1]).start()
+
+    @pl.when(sect == 1)
+    def _():
+        pltpu.make_async_copy(
+            tens_ref.at[0, :, pl.ds(half, half)], t1.at[:, pl.ds(0, half)], local_sem.at[1]
+        ).start()
+
+    barrier = pltpu.get_barrier_semaphore()
+
+    def greet(k, carry):
+        other = lax.rem(me + k, total)
+        pl.semaphore_signal(
+            barrier, inc=1, device_id=(other // ranks, lax.rem(other, ranks)), device_id_type=MESH
+        )
+        return carry
+
+    lax.fori_loop(1, total, greet, 0)
+
+    labels_copy.wait()
+    labels = jnp.broadcast_to(labels_v[...].reshape(1, count_blocks), (count_blocks, count_blocks))
+    place = lax.broadcasted_iota(jnp.int32, (count_blocks, count_blocks), 0)
+    charge = lax.broadcasted_iota(jnp.int32, (count_blocks, count_blocks), 1)
+    inv_v[...] = jnp.max(jnp.where(labels.T == charge, place, 0), axis=0, keepdims=True)
+    inv_copy = pltpu.make_async_copy(inv_v, inv_s, local_sem.at[2])
+    inv_copy.start()
+    bits_v[...] = jnp.zeros_like(bits_v)
+    bits_copy.wait()
+    bits_v[0:1, 0:rows] = bits_i[...].astype(jnp.float32)
+    inv_copy.wait()
+    left_copy.wait()
+    for i in range(count_blocks):
+        left_b[i] = left_v[:, i * block : (i + 1) * block]
+    for b in range(ranks):
+        for h in range(half):
+            where = inv_s[0, group * b + half * sect + h]
+            ordered[b, :, h * block : (h + 1) * block] = left_b[where]
+
+    pl.semaphore_wait(barrier, total - 1)
+
+    tens_to_one = pltpu.make_async_remote_copy(
+        src_ref=tens_ref.at[0, :, pl.ds(half, half)],
+        dst_ref=t0,
+        send_sem=tsend_sem.at[0],
+        recv_sem=trecv_sem.at[0],
+        device_id=(1, blk),
+        device_id_type=MESH,
+    )
+    tens_to_zero = pltpu.make_async_remote_copy(
+        src_ref=tens_ref.at[0, :, pl.ds(0, half + 1)],
+        dst_ref=t1,
+        send_sem=tsend_sem.at[1],
+        recv_sem=trecv_sem.at[1],
+        device_id=(0, blk),
+        device_id_type=MESH,
+    )
+    tens_back = pltpu.make_async_remote_copy(
+        src_ref=tens_ref.at[0, :, pl.ds(0, 1)],
+        dst_ref=t1.at[:, pl.ds(half, 1)],
+        send_sem=tsend_sem.at[2],
+        recv_sem=trecv_sem.at[2],
+        device_id=(1, lax.rem(blk + ranks - 1, ranks)),
+        device_id_type=MESH,
+    )
+
+    @pl.when(sect == 0)
+    def _():
+        tens_to_one.start()
+
+    @pl.when(sect == 1)
+    def _():
+        tens_to_zero.start()
+        tens_back.start()
+
+    mine = pl.ds(pl.multiple_of(blk * rows, rows), rows)
+
+    def send_left(k, carry):
+        other = lax.rem(blk + k, ranks)
+        pltpu.make_async_remote_copy(
+            src_ref=ordered.at[other],
+            dst_ref=state.at[mine],
+            send_sem=left_sem.at[0],
+            recv_sem=left_sem.at[1],
+            device_id=(sect, other),
+            device_id_type=MESH,
+        ).start()
+        return carry
+
+    lax.fori_loop(1, ranks, send_left, 0)
+    state[mine, :] = ordered[blk]
+
+    others = state.at[pl.ds(0, (ranks - 1) * rows)]
+    pltpu.make_async_copy(others, others, left_sem.at[1]).wait()
+
+    @pl.when(sect == 0)
+    def _():
+        pltpu.make_async_copy(tens_ref.at[0, :, pl.ds(0, half)], t0, local_sem.at[1]).wait()
+
+    @pl.when(sect == 1)
+    def _():
+        tens_to_one.wait_recv()
+
+    stays, raiseds = [], []
+    sum_stay = jnp.zeros((samples, block), jnp.float32)
+    sum_raised = jnp.zeros((samples, block), jnp.float32)
+    for h in range(half):
+        both = jnp.concatenate([t0[0, h], t0[1, h]], axis=1)
+        image = jnp.dot(
+            state[:, h * block : (h + 1) * block], both, preferred_element_type=jnp.float32
+        )
+        stay, raised = image[:, :block], image[:, block:]
+        stays.append(stay)
+        raiseds.append(raised)
+        sum_stay += stay * stay
+        sum_raised += raised * raised
+    norm_stay = jnp.sum(sum_stay, axis=1, keepdims=True)
+    norm_raised = jnp.sum(sum_raised, axis=1, keepdims=True)
+    scale_stay = lax.rsqrt(norm_stay / part_width + EPS)
+    scale_raised = lax.rsqrt(norm_raised / part_width + EPS)
+
+    @pl.when(sect == 0)
+    def _():
+        tens_to_zero.wait_recv()
+
+    @pl.when(sect == 1)
+    def _():
+        pltpu.make_async_copy(
+            tens_ref.at[0, :, pl.ds(half, half)], t1.at[:, pl.ds(0, half)], local_sem.at[1]
+        ).wait()
+        tens_back.wait_recv()
+
+    def halves(value):
+        high = value.astype(jnp.bfloat16)
+        low = (value - high.astype(jnp.float32)).astype(jnp.bfloat16)
+        return jnp.concatenate([high, low], axis=1)
+
+    sums = [[jnp.zeros((samples, block), jnp.float32) for _ in range(2)] for _ in range(2)]
+    for j in range(half + 1):
+        both = jnp.concatenate([t1[0, j], t1[1, j]], axis=1)
+        twice = jnp.concatenate([both, both], axis=0)
+        for first in range(2):
+            if (first == 0 and j == half) or (first == 1 and j == 0):
+                continue
+            value = raiseds[j - 1] * scale_raised if first else stays[j] * scale_stay
+            image = jnp.dot(halves(value), twice, preferred_element_type=jnp.float32)
+            for second in range(2):
+                piece = image[:, second * block : (second + 1) * block]
+                sums[first][second] += piece * piece
+    columns = [norm_stay, norm_raised]
+    for second in range(2):
+        for first in range(2):
+            columns.append(jnp.sum(sums[first][second], axis=1, keepdims=True))
+
+    lane = lax.broadcasted_iota(jnp.int32, (samples, block), 1)
+    row = lax.broadcasted_iota(jnp.int32, (samples, block), 0)
+    spread = jnp.zeros((samples, block), jnp.float32)
+    for v, column in enumerate(columns):
+        spread = jnp.where(lane // rows == v, column, spread)
+    spread = jnp.where(lane % rows == row % rows, spread, 0.0)
+    for b in range(ranks):
+        part[b] = jnp.sum(spread[b * rows : (b + 1) * rows], axis=0, keepdims=True)
+    own_bits = pltpu.roll(bits_v[...], 6 * rows, 1)[0:1]
+    part[blk] = part[blk] + jnp.where(sect == 0, own_bits, 0.0)
+
+    def send_part(k, carry):
+        other = lax.rem(me + k, total)
+        rank = lax.rem(other, ranks)
+        pltpu.make_async_remote_copy(
+            src_ref=part.at[rank],
+            dst_ref=inbox.at[k - 1],
+            send_sem=part_sem.at[0],
+            recv_sem=part_sem.at[1],
+            device_id=(other // ranks, rank),
+            device_id_type=MESH,
+        ).start()
+        return carry
+
+    lax.fori_loop(1, total, send_part, 0)
+    pltpu.make_async_copy(inbox, inbox, part_sem.at[1]).wait()
+    stack[0:1, :] = part[blk]
+    for k in range(total - 1):
+        stack[k + 1 : k + 2, :] = inbox[k]
+    all_parts = stack[...]
+    sums_all = jnp.sum(all_parts, axis=0, keepdims=True)
+    weight = (all_parts / part_width + EPS) / (sums_all / width + EPS)
+    lane = lax.broadcasted_iota(jnp.int32, (total, block), 1)
+    weight = jnp.where(
+        lane < 4 * rows, pltpu.roll(weight, 2 * rows, 1), pltpu.roll(weight, 4 * rows, 1)
+    )
+    later = jnp.sum(all_parts * weight, axis=0, keepdims=True)
+
+    def value(source, v):
+        wide = jnp.broadcast_to(source, (8, block))
+        return wide if v == 0 else pltpu.roll(wide, block - v * rows, 1)
+
+    bit0 = value(sums_all, 6) == 1.0
+    bit1 = bits_v[...] == 1.0
+    zero, one = value(sums_all, 0), value(sums_all, 1)
+    prob0 = jnp.where(bit0, one, zero) / (zero + one)
+    zero = jnp.where(bit0, value(later, 3), value(later, 2))
+    one = jnp.where(bit0, value(later, 5), value(later, 4))
+    prob1 = jnp.where(bit1, one, zero) / (zero + one)
+    log0 = jnp.log(prob0)
+    log1 = log0 + jnp.log(prob1)
+    prob_ref[...] = jnp.where(sect == 0, prob0, prob1)[0:1, 0:rows]
+    log_ref[...] = jnp.where(sect == 0, log0, log1)[0:1, 0:rows]
+
+    pltpu.make_async_copy(others, others, left_sem.at[0]).wait()
+    pltpu.make_async_copy(inbox, inbox, part_sem.at[0]).wait()
+
+    @pl.when(sect == 0)
+    def _():
+        tens_to_one.wait_send()
+
+    @pl.when(sect == 1)
+    def _():
+        tens_to_zero.wait_send()
+        tens_back.wait_send()
+
+
+def body_pair(ranks, bits, labels, left, tensors):
+    rows = bits.shape[1]
+    count_blocks = labels.shape[0]
+    block = tensors.shape[-1]
+    group = tensors.shape[2]
+    half = group // 2
+    vmem = pl.BlockSpec(memory_space=pltpu.VMEM)
+    hbm = pl.BlockSpec(memory_space=pl.ANY)
+    out = jax.ShapeDtypeStruct(bits.shape, jnp.float32)
+    return pl.pallas_call(
+        functools.partial(pair_kernel, ranks),
+        out_shape=(out, out),
+        in_specs=[hbm, hbm, hbm, hbm],
+        out_specs=(vmem, vmem),
+        scratch_shapes=[
+            pltpu.VMEM(bits.shape, jnp.int32),
+            pltpu.VMEM(labels.shape, jnp.int32),
+            pltpu.VMEM(left.shape, jnp.bfloat16),
+            pltpu.VMEM((count_blocks, rows, block), jnp.bfloat16),
+            pltpu.VMEM((1, count_blocks), jnp.int32),
+            pltpu.SMEM((1, count_blocks), jnp.int32),
+            pltpu.VMEM((ranks, rows, half * block), jnp.bfloat16),
+            pltpu.VMEM((ranks * rows, half * block), jnp.bfloat16),
+            pltpu.VMEM((2, half, block, block), jnp.bfloat16),
+            pltpu.VMEM((2, half + 1, block, block), jnp.bfloat16),
+            pltpu.VMEM((ranks, 1, block), jnp.float32),
+            pltpu.VMEM((2 * ranks - 1, 1, block), jnp.float32),
+            pltpu.VMEM((2 * ranks, block), jnp.float32),
+            pltpu.VMEM((8, block), jnp.float32),
+            pltpu.SemaphoreType.DMA((5,)),
+            pltpu.SemaphoreType.DMA((3,)),
+            pltpu.SemaphoreType.DMA((3,)),
+            pltpu.SemaphoreType.DMA((2,)),
+            pltpu.SemaphoreType.DMA((2,)),
+        ],
+        compiler_params=pltpu.CompilerParams(
+            collective_id=0, has_side_effects=True, vmem_limit_bytes=60 * 1024 * 1024
+        ),
+        name="score_pair",
+    )(bits, labels, left, tensors)
 
 
 def solution(mesh):
     in_specs = (P("sect", "blk"), P(), P("blk", None), P("sect", None, "blk", None, None))
     out_specs = (P("sect", "blk"), P("sect", "blk"))
+    if mesh.shape["sect"] == 2:
+        body = functools.partial(body_pair, mesh.shape["blk"])
+    else:
+        body = body_many
     return jax.shard_map(body, mesh=mesh, in_specs=in_specs, out_specs=out_specs, check_vma=False)

time: 168 us -> 24.4 us (0.15)
  waiting for transfers between devices: 117 us -> 0 us
  Pallas kernels: 0 us -> 21.8 us
  matrix products: 13.9 us -> 0 us
  between operations: 14.1 us -> 0.65 us
  starting transfers between devices: 10.5 us -> 0 us
  other arithmetic: 5.3 us -> 0 us
  local copies, waits for them, and re-layouts: 6.62 us -> 1.8 us
    all_gather x1 -> x0, waiting for transfers between devices: 74.7 us -> none  [body(): whole = lax.all_gather(tensors, 'blk', axis=2, tiled=True)[0]]
    ppermute x4 -> x0, waiting for transfers between devices: 42.1 us -> none  [passed_along(): lax.ppermute(value, axis, [(source, source + steps) for source in range(f...]
    pallas_call x0 -> x1, Pallas kernels: none -> 21.8 us  [body_pair(): pl.pallas_call(functools.partial(pair_kernel, ranks), out_shape=(out, out...]
    dot_general x3 -> x0, matrix products: 13.9 us -> none  [the longest x2 12.9 us: site_images(): jnp.einsum('rck,bckl->brcl', blocks, weights, preferred_element_type=jnp....]
    ppermute x4 -> x0, starting transfers between devices: 10.5 us -> none  [passed_along(): lax.ppermute(value, axis, [(source, source + steps) for source in range(f...]
    while x2 -> x0, other arithmetic: 2.66 us -> none
    unnamed x9 -> x6, local copies, waits for them, and re-layouts: 4.15 us -> 1.8 us
  transfers between devices with their start and end apart: 5 -> 0, of which waited for: 3 -> 0; matrix products, arithmetic and copies ran while one was open for 2% -> 0% of each run, Pallas kernels for 0% -> 0%
where the time goes in v1:
time: 24.4 us; the launch traced here: 24.2 us
  Pallas kernels  21.8 us (89%)
  local copies, waits for them, and re-layouts  1.8 us (7%)
  between operations  0.65 us (3%)
    pallas_call x1, Pallas kernels, body_pair(): pl.pallas_call(functools.partial(pair_kernel, ranks), out_shape=(out, out...  21.8 us
    unnamed x6, local copies, waits for them, and re-layouts  1.8 us

profile of v1, /device:TPU:0, one launch (start us, length us, event | category | flops | bytes accessed | tf_op | source)
XLA Modules:
  0.0 24.2 jit_solution(119738304032429587)
XLA Ops:
  0.6 21.8 %score_pair.1 = (f32[1,16]{1,0:T(1,128)}, f32[1,16]{1,0:T(1,128)}) custom-call(s32[1,16]{1,0:T(1,128)} %bits_ref.1, s32[128]{0:T(128)} %labels_ref.1, bf16[16,16384]{1,0:T(8,128)(2,1)} %left_ref.1, bf16[1,2,8,128,128]{4,3,2,1,0:T(8,128)(2,1)} %tens_ref.1), custom_call_target="tpu_custom_call" | custom-call | tf_op jit(solution)/shard_map/score_pair/pallas_call | solution.py:380
  22.4 0.0 copy-start.1
  22.4 0.7 %copy-done.1 = f32[1,16]{1,0:T(1,128)S(1)} copy-done((f32[1,16]{1,0:T(1,128)S(1)}, f32[1,16]{1,0:T(1,128)}, u32[]{:S(2)}) %copy-start.1) | copy-done | bytes 88
  23.1 0.0 copy-start
  23.1 0.5 %copy.8 = f32[1,16]{1,0:T(1,128)} copy(f32[1,16]{1,0:T(1,128)S(1)} %copy-done.1) | data formatting | bytes 128
  23.6 0.1 copy-done
  23.7 0.5 %copy.9 = f32[1,16]{1,0:T(1,128)} copy(f32[1,16]{1,0:T(1,128)S(1)} %copy-done) | data formatting | bytes 128
Async XLA Ops:
  22.4 0.7 %copy-start.1 = (f32[1,16]{1,0:T(1,128)S(1)}, f32[1,16]{1,0:T(1,128)}, u32[]{:S(2)}) copy-start(f32[1,16]{1,0:T(1,128)} %get-tuple-element.4) | copy-start | bytes 196
  23.1 0.6 %copy-start = (f32[1,16]{1,0:T(1,128)S(1)}, f32[1,16]{1,0:T(1,128)}, u32[]{:S(2)}) copy-start(f32[1,16]{1,0:T(1,128)} %get-tuple-element.5) | copy-start | bytes 196

commit v2 on v1

--- a/solution.py
+++ b/solution.py
@@ -104,8 +104,7 @@
     labels_ref,
     left_ref,
     tens_ref,
-    prob_ref,
-    log_ref,
+    out_ref,
     bits_i,
     labels_v,
     left_v,
@@ -114,15 +113,19 @@
     inv_s,
     ordered,
     state,
+    images,
     t0,
     t1,
-    part,
+    part0,
+    part1,
     inbox,
     stack,
     bits_v,
     local_sem,
-    tsend_sem,
-    trecv_sem,
+    t0_send,
+    t0_recv,
+    t1_send,
+    t1_recv,
     left_sem,
     part_sem,
 ):
@@ -141,20 +144,22 @@
 
     labels_copy = pltpu.make_async_copy(labels_ref, labels_v, local_sem.at[3])
     labels_copy.start()
+    left_copy = pltpu.make_async_copy(left_ref, left_v, local_sem.at[0])
+    left_copy.start()
     bits_copy = pltpu.make_async_copy(bits_ref, bits_i, local_sem.at[4])
     bits_copy.start()
-    left_copy = pltpu.make_async_copy(left_ref, left_v, local_sem.at[0])
-    left_copy.start()
+    own_t0 = pltpu.make_async_copy(tens_ref.at[0, :, pl.ds(0, half)], t0, local_sem.at[1])
+    own_t1 = pltpu.make_async_copy(
+        tens_ref.at[0, :, pl.ds(half, half)], t1.at[:, pl.ds(0, half)], local_sem.at[1]
+    )
 
     @pl.when(sect == 0)
     def _():
-        pltpu.make_async_copy(tens_ref.at[0, :, pl.ds(0, half)], t0, local_sem.at[1]).start()
+        own_t0.start()
 
     @pl.when(sect == 1)
     def _():
-        pltpu.make_async_copy(
-            tens_ref.at[0, :, pl.ds(half, half)], t1.at[:, pl.ds(0, half)], local_sem.at[1]
-        ).start()
+        own_t1.start()
 
     barrier = pltpu.get_barrier_semaphore()
 
@@ -174,54 +179,60 @@
     inv_v[...] = jnp.max(jnp.where(labels.T == charge, place, 0), axis=0, keepdims=True)
     inv_copy = pltpu.make_async_copy(inv_v, inv_s, local_sem.at[2])
     inv_copy.start()
+    left_copy.wait()
+    for i in range(count_blocks):
+        left_b[i] = left_v[:, i * block : (i + 1) * block]
     bits_v[...] = jnp.zeros_like(bits_v)
     bits_copy.wait()
     bits_v[0:1, 0:rows] = bits_i[...].astype(jnp.float32)
+
+    pl.semaphore_wait(barrier, total - 1)
+
+    def tens_to_one(h):
+        return pltpu.make_async_remote_copy(
+            src_ref=tens_ref.at[0, :, pl.ds(half + h, 1)],
+            dst_ref=t0.at[:, pl.ds(h, 1)],
+            send_sem=t0_send.at[h],
+            recv_sem=t0_recv.at[h],
+            device_id=(1, blk),
+            device_id_type=MESH,
+        )
+
+    def tens_to_zero(j):
+        return pltpu.make_async_remote_copy(
+            src_ref=tens_ref.at[0, :, pl.ds(j, 1)],
+            dst_ref=t1.at[:, pl.ds(j, 1)],
+            send_sem=t1_send.at[j],
+            recv_sem=t1_recv.at[j],
+            device_id=(0, blk),
+            device_id_type=MESH,
+        )
+
+    tens_back = pltpu.make_async_remote_copy(
+        src_ref=tens_ref.at[0, :, pl.ds(0, 1)],
+        dst_ref=t1.at[:, pl.ds(half, 1)],
+        send_sem=t1_send.at[half + 1],
+        recv_sem=t1_recv.at[half],
+        device_id=(1, lax.rem(blk + ranks - 1, ranks)),
+        device_id_type=MESH,
+    )
+
+    @pl.when(sect == 0)
+    def _():
+        for h in range(half):
+            tens_to_one(h).start()
+
+    @pl.when(sect == 1)
+    def _():
+        for j in range(half + 1):
+            tens_to_zero(j).start()
+        tens_back.start()
+
     inv_copy.wait()
-    left_copy.wait()
-    for i in range(count_blocks):
-        left_b[i] = left_v[:, i * block : (i + 1) * block]
     for b in range(ranks):
         for h in range(half):
             where = inv_s[0, group * b + half * sect + h]
             ordered[b, :, h * block : (h + 1) * block] = left_b[where]
-
-    pl.semaphore_wait(barrier, total - 1)
-
-    tens_to_one = pltpu.make_async_remote_copy(
-        src_ref=tens_ref.at[0, :, pl.ds(half, half)],
-        dst_ref=t0,
-        send_sem=tsend_sem.at[0],
-        recv_sem=trecv_sem.at[0],
-        device_id=(1, blk),
-        device_id_type=MESH,
-    )
-    tens_to_zero = pltpu.make_async_remote_copy(
-        src_ref=tens_ref.at[0, :, pl.ds(0, half + 1)],
-        dst_ref=t1,
-        send_sem=tsend_sem.at[1],
-        recv_sem=trecv_sem.at[1],
-        device_id=(0, blk),
-        device_id_type=MESH,
-    )
-    tens_back = pltpu.make_async_remote_copy(
-        src_ref=tens_ref.at[0, :, pl.ds(0, 1)],
-        dst_ref=t1.at[:, pl.ds(half, 1)],
-        send_sem=tsend_sem.at[2],
-        recv_sem=trecv_sem.at[2],
-        device_id=(1, lax.rem(blk + ranks - 1, ranks)),
-        device_id_type=MESH,
-    )
-
-    @pl.when(sect == 0)
-    def _():
-        tens_to_one.start()
-
-    @pl.when(sect == 1)
-    def _():
-        tens_to_zero.start()
-        tens_back.start()
-
     mine = pl.ds(pl.multiple_of(blk * rows, rows), rows)
 
     def send_left(k, carry):
@@ -244,54 +255,85 @@
 
     @pl.when(sect == 0)
     def _():
-        pltpu.make_async_copy(tens_ref.at[0, :, pl.ds(0, half)], t0, local_sem.at[1]).wait()
-
-    @pl.when(sect == 1)
-    def _():
-        tens_to_one.wait_recv()
-
-    stays, raiseds = [], []
+        own_t0.wait()
+
     sum_stay = jnp.zeros((samples, block), jnp.float32)
     sum_raised = jnp.zeros((samples, block), jnp.float32)
     for h in range(half):
+
+        @pl.when(sect == 1)
+        def _():
+            tens_to_one(h).wait_recv()
+
         both = jnp.concatenate([t0[0, h], t0[1, h]], axis=1)
         image = jnp.dot(
             state[:, h * block : (h + 1) * block], both, preferred_element_type=jnp.float32
         )
+        images[h] = image
         stay, raised = image[:, :block], image[:, block:]
-        stays.append(stay)
-        raiseds.append(raised)
         sum_stay += stay * stay
         sum_raised += raised * raised
     norm_stay = jnp.sum(sum_stay, axis=1, keepdims=True)
     norm_raised = jnp.sum(sum_raised, axis=1, keepdims=True)
-    scale_stay = lax.rsqrt(norm_stay / part_width + EPS)
-    scale_raised = lax.rsqrt(norm_raised / part_width + EPS)
-
-    @pl.when(sect == 0)
-    def _():
-        tens_to_zero.wait_recv()
-
-    @pl.when(sect == 1)
-    def _():
-        pltpu.make_async_copy(
-            tens_ref.at[0, :, pl.ds(half, half)], t1.at[:, pl.ds(0, half)], local_sem.at[1]
-        ).wait()
-        tens_back.wait_recv()
+
+    lane = lax.broadcasted_iota(jnp.int32, (samples, block), 1)
+    row = lax.broadcasted_iota(jnp.int32, (samples, block), 0)
+
+    def fill(part, columns):
+        spread = jnp.zeros((samples, block), jnp.float32)
+        for v, column in enumerate(columns):
+            spread = jnp.where(lane // rows == v, column, spread)
+        spread = jnp.where(lane % rows == row % rows, spread, 0.0)
+        for b in range(ranks):
+            part[b] = jnp.sum(spread[b * rows : (b + 1) * rows], axis=0, keepdims=True)
+
+    def send_part(part, target):
+        def one(k, carry):
+            rank = lax.rem(blk + k, ranks)
+            slot = lax.rem(target * ranks + rank - me + total, total) - 1
+            pltpu.make_async_remote_copy(
+                src_ref=part.at[rank],
+                dst_ref=inbox.at[slot],
+                send_sem=part_sem.at[0],
+                recv_sem=part_sem.at[1],
+                device_id=(target, rank),
+                device_id_type=MESH,
+            ).start()
+            return carry
+
+        lax.fori_loop(jnp.where(sect == target, 1, 0), ranks, one, 0)
+
+    fill(part0, [norm_stay, norm_raised])
+    send_part(part0, 0)
+
+    scales = [lax.rsqrt(norm_stay / part_width + EPS), lax.rsqrt(norm_raised / part_width + EPS)]
 
     def halves(value):
         high = value.astype(jnp.bfloat16)
         low = (value - high.astype(jnp.float32)).astype(jnp.bfloat16)
         return jnp.concatenate([high, low], axis=1)
 
+    @pl.when(sect == 1)
+    def _():
+        own_t1.wait()
+
     sums = [[jnp.zeros((samples, block), jnp.float32) for _ in range(2)] for _ in range(2)]
     for j in range(half + 1):
+        if j == half:
+            tens_to_zero(j).wait_recv()
+        else:
+
+            @pl.when(sect == 0)
+            def _():
+                tens_to_zero(j).wait_recv()
+
         both = jnp.concatenate([t1[0, j], t1[1, j]], axis=1)
         twice = jnp.concatenate([both, both], axis=0)
         for first in range(2):
-            if (first == 0 and j == half) or (first == 1 and j == 0):
+            source = j - first
+            if source < 0 or source == half:
                 continue
-            value = raiseds[j - 1] * scale_raised if first else stays[j] * scale_stay
+            value = images[source, :, first * block : (first + 1) * block] * scales[first]
             image = jnp.dot(halves(value), twice, preferred_element_type=jnp.float32)
             for second in range(2):
                 piece = image[:, second * block : (second + 1) * block]
@@ -300,71 +342,59 @@
     for second in range(2):
         for first in range(2):
             columns.append(jnp.sum(sums[first][second], axis=1, keepdims=True))
-
-    lane = lax.broadcasted_iota(jnp.int32, (samples, block), 1)
-    row = lax.broadcasted_iota(jnp.int32, (samples, block), 0)
-    spread = jnp.zeros((samples, block), jnp.float32)
-    for v, column in enumerate(columns):
-        spread = jnp.where(lane // rows == v, column, spread)
-    spread = jnp.where(lane % rows == row % rows, spread, 0.0)
-    for b in range(ranks):
-        part[b] = jnp.sum(spread[b * rows : (b + 1) * rows], axis=0, keepdims=True)
+    fill(part1, columns)
     own_bits = pltpu.roll(bits_v[...], 6 * rows, 1)[0:1]
-    part[blk] = part[blk] + jnp.where(sect == 0, own_bits, 0.0)
-
-    def send_part(k, carry):
-        other = lax.rem(me + k, total)
-        rank = lax.rem(other, ranks)
-        pltpu.make_async_remote_copy(
-            src_ref=part.at[rank],
-            dst_ref=inbox.at[k - 1],
-            send_sem=part_sem.at[0],
-            recv_sem=part_sem.at[1],
-            device_id=(other // ranks, rank),
-            device_id_type=MESH,
-        ).start()
-        return carry
-
-    lax.fori_loop(1, total, send_part, 0)
+    part1[blk] = part1[blk] + jnp.where(sect == 0, own_bits, 0.0)
+    send_part(part1, 1)
+
     pltpu.make_async_copy(inbox, inbox, part_sem.at[1]).wait()
-    stack[0:1, :] = part[blk]
+    stack[0:1, :] = jnp.where(sect == 0, part0[blk], part1[blk])
     for k in range(total - 1):
         stack[k + 1 : k + 2, :] = inbox[k]
     all_parts = stack[...]
     sums_all = jnp.sum(all_parts, axis=0, keepdims=True)
-    weight = (all_parts / part_width + EPS) / (sums_all / width + EPS)
-    lane = lax.broadcasted_iota(jnp.int32, (total, block), 1)
-    weight = jnp.where(
-        lane < 4 * rows, pltpu.roll(weight, 2 * rows, 1), pltpu.roll(weight, 4 * rows, 1)
-    )
-    later = jnp.sum(all_parts * weight, axis=0, keepdims=True)
+    here = bits_v[...] == 1.0
 
     def value(source, v):
         wide = jnp.broadcast_to(source, (8, block))
         return wide if v == 0 else pltpu.roll(wide, block - v * rows, 1)
 
-    bit0 = value(sums_all, 6) == 1.0
-    bit1 = bits_v[...] == 1.0
-    zero, one = value(sums_all, 0), value(sums_all, 1)
-    prob0 = jnp.where(bit0, one, zero) / (zero + one)
-    zero = jnp.where(bit0, value(later, 3), value(later, 2))
-    one = jnp.where(bit0, value(later, 5), value(later, 4))
-    prob1 = jnp.where(bit1, one, zero) / (zero + one)
-    log0 = jnp.log(prob0)
-    log1 = log0 + jnp.log(prob1)
-    prob_ref[...] = jnp.where(sect == 0, prob0, prob1)[0:1, 0:rows]
-    log_ref[...] = jnp.where(sect == 0, log0, log1)[0:1, 0:rows]
+    norm_zero, norm_one = value(sums_all, 0), value(sums_all, 1)
+
+    @pl.when(sect == 0)
+    def _():
+        prob = jnp.where(here, norm_one, norm_zero) / (norm_zero + norm_one)
+        out_ref[0:1, :] = prob[0:1]
+        out_ref[1:2, :] = jnp.log(prob)[0:1]
+
+    @pl.when(sect == 1)
+    def _():
+        weight = (all_parts / part_width + EPS) / (sums_all / width + EPS)
+        where = lax.broadcasted_iota(jnp.int32, (total, block), 1)
+        weight = jnp.where(
+            where < 4 * rows, pltpu.roll(weight, 2 * rows, 1), pltpu.roll(weight, 4 * rows, 1)
+        )
+        later = jnp.sum(all_parts * weight, axis=0, keepdims=True)
+        before = value(sums_all, 6) == 1.0
+        prob0 = jnp.where(before, norm_one, norm_zero) / (norm_zero + norm_one)
+        zero = jnp.where(before, value(later, 3), value(later, 2))
+        one = jnp.where(before, value(later, 5), value(later, 4))
+        prob = jnp.where(here, one, zero) / (zero + one)
+        out_ref[0:1, :] = prob[0:1]
+        out_ref[1:2, :] = (jnp.log(prob0) + jnp.log(prob))[0:1]
 
     pltpu.make_async_copy(others, others, left_sem.at[0]).wait()
     pltpu.make_async_copy(inbox, inbox, part_sem.at[0]).wait()
 
     @pl.when(sect == 0)
     def _():
-        tens_to_one.wait_send()
+        for h in range(half):
+            tens_to_one(h).wait_send()
 
     @pl.when(sect == 1)
     def _():
-        tens_to_zero.wait_send()
+        for j in range(half + 1):
+            tens_to_zero(j).wait_send()
         tens_back.wait_send()
 
 
@@ -376,12 +406,12 @@
     half = group // 2
     vmem = pl.BlockSpec(memory_space=pltpu.VMEM)
     hbm = pl.BlockSpec(memory_space=pl.ANY)
-    out = jax.ShapeDtypeStruct(bits.shape, jnp.float32)
-    return pl.pallas_call(
+    dma = pltpu.SemaphoreType.DMA
+    scored = pl.pallas_call(
         functools.partial(pair_kernel, ranks),
-        out_shape=(out, out),
+        out_shape=jax.ShapeDtypeStruct((2, block), jnp.float32),
         in_specs=[hbm, hbm, hbm, hbm],
-        out_specs=(vmem, vmem),
+        out_specs=vmem,
         scratch_shapes=[
             pltpu.VMEM(bits.shape, jnp.int32),
             pltpu.VMEM(labels.shape, jnp.int32),
@@ -391,23 +421,28 @@
             pltpu.SMEM((1, count_blocks), jnp.int32),
             pltpu.VMEM((ranks, rows, half * block), jnp.bfloat16),
             pltpu.VMEM((ranks * rows, half * block), jnp.bfloat16),
+            pltpu.VMEM((half, ranks * rows, 2 * block), jnp.float32),
             pltpu.VMEM((2, half, block, block), jnp.bfloat16),
             pltpu.VMEM((2, half + 1, block, block), jnp.bfloat16),
+            pltpu.VMEM((ranks, 1, block), jnp.float32),
             pltpu.VMEM((ranks, 1, block), jnp.float32),
             pltpu.VMEM((2 * ranks - 1, 1, block), jnp.float32),
             pltpu.VMEM((2 * ranks, block), jnp.float32),
             pltpu.VMEM((8, block), jnp.float32),
-            pltpu.SemaphoreType.DMA((5,)),
-            pltpu.SemaphoreType.DMA((3,)),
-            pltpu.SemaphoreType.DMA((3,)),
-            pltpu.SemaphoreType.DMA((2,)),
-            pltpu.SemaphoreType.DMA((2,)),
+            dma((5,)),
+            dma((half,)),
+            dma((half,)),
+            dma((half + 2,)),
+            dma((half + 1,)),
+            dma((2,)),
+            dma((2,)),
         ],
         compiler_params=pltpu.CompilerParams(
             collective_id=0, has_side_effects=True, vmem_limit_bytes=60 * 1024 * 1024
         ),
         name="score_pair",
     )(bits, labels, left, tensors)
+    return scored[0:1, :rows], scored[1:2, :rows]
 
 
 def solution(mesh):

time: 24.4 us -> 23.9 us (0.980)
  local copies, waits for them, and re-layouts: 1.8 us -> 1.25 us
    unnamed x6 -> x0, local copies, waits for them, and re-layouts: 1.8 us -> none
    slice x0 -> x1, local copies, waits for them, and re-layouts: none -> 1.25 us  [body_pair(): return (scored[0:1, :rows], scored[1:2, :rows])]
where the time goes in v2:
time: 23.9 us; the launch traced here: 23.8 us
  Pallas kernels  21.9 us (92%)
  local copies, waits for them, and re-layouts  1.25 us (5%)
  between operations  0.64 us (3%)
    pallas_call x1, Pallas kernels, body_pair(): pl.pallas_call(functools.partial(pair_kernel, ranks), out_shape=jax.Shape...  21.9 us
    slice x1, local copies, waits for them, and re-layouts, body_pair(): return (scored[0:1, :rows], scored[1:2, :rows])  1.25 us

profile of v2, /device:TPU:0, one launch (start us, length us, event | category | flops | bytes accessed | tf_op | source)
XLA Modules:
  0.0 23.8 jit_solution(7675641583912504651)
XLA Ops:
  0.6 21.9 %score_pair.1 = f32[2,128]{1,0:T(2,128)} custom-call(s32[1,16]{1,0:T(1,128)} %bits_ref.1, s32[128]{0:T(128)} %labels_ref.1, bf16[16,16384]{1,0:T(8,128)(2,1)} %left_ref.1, bf16[1,2,8,128,128]{4,3,2,1,0:T(8,128)(2,1)} %tens_ref.1), custom_call_target="tpu_custom_call" | custom-call | tf_op jit(solution)/shard_map/score_pair/pallas_call | solution.py:410
  22.5 1.3 %fusion = (f32[1,16]{1,0:T(1,128)}, f32[1,16]{1,0:T(1,128)}) fusion(f32[2,128]{1,0:T(2,128)} %score_pair.1), kind=kLoop, calls=%fused_computation | loop fusion | bytes 256 | tf_op jit(solution)/shard_map/slice | solution.py:445

commit v3 on v2

--- a/solution.py
+++ b/solution.py
@@ -185,6 +185,11 @@
     bits_v[...] = jnp.zeros_like(bits_v)
     bits_copy.wait()
     bits_v[0:1, 0:rows] = bits_i[...].astype(jnp.float32)
+    inv_copy.wait()
+    for b in range(ranks):
+        for h in range(half):
+            where = inv_s[0, group * b + half * sect + h]
+            ordered[b, :, h * block : (h + 1) * block] = left_b[where]
 
     pl.semaphore_wait(barrier, total - 1)
 
@@ -217,25 +222,9 @@
         device_id_type=MESH,
     )
 
-    @pl.when(sect == 0)
-    def _():
-        for h in range(half):
-            tens_to_one(h).start()
-
-    @pl.when(sect == 1)
-    def _():
-        for j in range(half + 1):
-            tens_to_zero(j).start()
-        tens_back.start()
-
-    inv_copy.wait()
-    for b in range(ranks):
-        for h in range(half):
-            where = inv_s[0, group * b + half * sect + h]
-            ordered[b, :, h * block : (h + 1) * block] = left_b[where]
     mine = pl.ds(pl.multiple_of(blk * rows, rows), rows)
 
-    def send_left(k, carry):
+    def send_left(k):
         other = lax.rem(blk + k, ranks)
         pltpu.make_async_remote_copy(
             src_ref=ordered.at[other],
@@ -245,9 +234,25 @@
             device_id=(sect, other),
             device_id_type=MESH,
         ).start()
-        return carry
-
-    lax.fori_loop(1, ranks, send_left, 0)
+
+    far_first = sorted(range(1, ranks), key=lambda k: abs(k - ranks // 2))
+    for i, k in enumerate(far_first):
+        send_left(k)
+        if i % 2 == 1 and i // 2 < half:
+
+            @pl.when(sect == 0)
+            def _():
+                tens_to_one(i // 2).start()
+
+            @pl.when(sect == 1)
+            def _():
+                tens_to_zero(i // 2).start()
+
+    @pl.when(sect == 1)
+    def _():
+        tens_to_zero(half).start()
+        tens_back.start()
+
     state[mine, :] = ordered[blk]
 
     others = state.at[pl.ds(0, (ranks - 1) * rows)]
@@ -409,7 +414,7 @@
     dma = pltpu.SemaphoreType.DMA
     scored = pl.pallas_call(
         functools.partial(pair_kernel, ranks),
-        out_shape=jax.ShapeDtypeStruct((2, block), jnp.float32),
+        out_shape=pltpu.VMEM((2, block), jnp.float32),
         in_specs=[hbm, hbm, hbm, hbm],
         out_specs=vmem,
         scratch_shapes=[

time: 23.9 us -> 22.1 us (0.925)
  Pallas kernels: 21.9 us -> 20.8 us
  local copies, waits for them, and re-layouts: 1.25 us -> 0.52 us
    pallas_call x1, Pallas kernels: 21.9 us -> 20.8 us  [body_pair(): pl.pallas_call(functools.partial(pair_kernel, ranks), out_shape=pltpu.VME...]
    slice x1, local copies, waits for them, and re-layouts: 1.25 us -> 0.52 us  [body_pair(): return (scored[0:1, :rows], scored[1:2, :rows])]
where the time goes in v3:
time: 22.1 us; the launch traced here: 21.9 us
  Pallas kernels  20.8 us (94%)
  between operations  0.64 us (3%)
  local copies, waits for them, and re-layouts  0.52 us (2%)
    pallas_call x1, Pallas kernels, body_pair(): pl.pallas_call(functools.partial(pair_kernel, ranks), out_shape=pltpu.VME...  20.8 us
    slice x1, local copies, waits for them, and re-layouts, body_pair(): return (scored[0:1, :rows], scored[1:2, :rows])  0.52 us

profile of v3, /device:TPU:0, one launch (start us, length us, event | category | flops | bytes accessed | tf_op | source)
XLA Modules:
  0.0 21.9 jit_solution(1896921080386785220)
XLA Ops:
  0.6 20.8 %score_pair.1 = f32[2,128]{1,0:T(2,128)S(1)} custom-call(s32[1,16]{1,0:T(1,128)} %bits_ref.1, s32[128]{0:T(128)} %labels_ref.1, bf16[16,16384]{1,0:T(8,128)(2,1)} %left_ref.1, bf16[1,2,8,128,128]{4,3,2,1,0:T(8,128)(2,1)} %tens_ref.1), custom_call_target="tpu_custom_call" | custom-call | tf_op jit(solution)/shard_map/score_pair/pallas_call | solution.py:415
  21.4 0.5 %fusion = (f32[1,16]{1,0:T(1,128)}, f32[1,16]{1,0:T(1,128)}) fusion(f32[2,128]{1,0:T(2,128)S(1)} %score_pair.1), kind=kLoop, calls=%fused_computation | loop fusion | bytes 256 | tf_op jit(solution)/shard_map/slice | solution.py:450

commit v4 on v3

--- a/solution.py
+++ b/solution.py
@@ -163,14 +163,13 @@
 
     barrier = pltpu.get_barrier_semaphore()
 
-    def greet(k, carry):
-        other = lax.rem(me + k, total)
+    far_first = sorted(range(1, ranks), key=lambda k: abs(k - ranks // 2))
+
+    pl.semaphore_signal(barrier, inc=1, device_id=(1 - sect, blk), device_id_type=MESH)
+    for k in far_first:
         pl.semaphore_signal(
-            barrier, inc=1, device_id=(other // ranks, lax.rem(other, ranks)), device_id_type=MESH
-        )
-        return carry
-
-    lax.fori_loop(1, total, greet, 0)
+            barrier, inc=1, device_id=(sect, lax.rem(blk + k, ranks)), device_id_type=MESH
+        )
 
     labels_copy.wait()
     labels = jnp.broadcast_to(labels_v[...].reshape(1, count_blocks), (count_blocks, count_blocks))
@@ -191,7 +190,7 @@
             where = inv_s[0, group * b + half * sect + h]
             ordered[b, :, h * block : (h + 1) * block] = left_b[where]
 
-    pl.semaphore_wait(barrier, total - 1)
+    pl.semaphore_wait(barrier, ranks)
 
     def tens_to_one(h):
         return pltpu.make_async_remote_copy(
@@ -235,7 +234,6 @@
             device_id_type=MESH,
         ).start()
 
-    far_first = sorted(range(1, ranks), key=lambda k: abs(k - ranks // 2))
     for i, k in enumerate(far_first):
         send_left(k)
         if i % 2 == 1 and i // 2 < half:
@@ -293,7 +291,7 @@
             part[b] = jnp.sum(spread[b * rows : (b + 1) * rows], axis=0, keepdims=True)
 
     def send_part(part, target):
-        def one(k, carry):
+        def one(k):
             rank = lax.rem(blk + k, ranks)
             slot = lax.rem(target * ranks + rank - me + total, total) - 1
             pltpu.make_async_remote_copy(
@@ -304,9 +302,13 @@
                 device_id=(target, rank),
                 device_id_type=MESH,
             ).start()
-            return carry
-
-        lax.fori_loop(jnp.where(sect == target, 1, 0), ranks, one, 0)
+
+        for k in far_first:
+            one(k)
+
+        @pl.when(sect != target)
+        def _():
+            one(0)
 
     fill(part0, [norm_stay, norm_raised])
     send_part(part0, 0)
@@ -334,14 +336,21 @@
 
         both = jnp.concatenate([t1[0, j], t1[1, j]], axis=1)
         twice = jnp.concatenate([both, both], axis=0)
-        for first in range(2):
-            source = j - first
-            if source < 0 or source == half:
-                continue
-            value = images[source, :, first * block : (first + 1) * block] * scales[first]
-            image = jnp.dot(halves(value), twice, preferred_element_type=jnp.float32)
+        firsts = [first for first in range(2) if 0 <= j - first < half]
+        values = [
+            images[j - first, :, first * block : (first + 1) * block] * scales[first]
+            for first in firsts
+        ]
+        image = jnp.dot(
+            jnp.concatenate([halves(value) for value in values], axis=0),
+            twice,
+            preferred_element_type=jnp.float32,
+        )
+        for i, first in enumerate(firsts):
             for second in range(2):
-                piece = image[:, second * block : (second + 1) * block]
+                piece = image[
+                    i * samples : (i + 1) * samples, second * block : (second + 1) * block
+                ]
                 sums[first][second] += piece * piece
     columns = [norm_stay, norm_raised]
     for second in range(2):

time: 22.1 us -> 21.2 us (0.959)
  Pallas kernels: 20.8 us -> 19.9 us
    pallas_call x1, Pallas kernels: 20.8 us -> 19.9 us  [body_pair(): pl.pallas_call(functools.partial(pair_kernel, ranks), out_shape=pltpu.VME...]
where the time goes in v4:
time: 21.2 us; the launch traced here: 21.1 us
  Pallas kernels  19.9 us (94%)
  between operations  0.64 us (3%)
  local copies, waits for them, and re-layouts  0.52 us (2%)
    pallas_call x1, Pallas kernels, body_pair(): pl.pallas_call(functools.partial(pair_kernel, ranks), out_shape=pltpu.VME...  19.9 us
    slice x1, local copies, waits for them, and re-layouts, body_pair(): return (scored[0:1, :rows], scored[1:2, :rows])  0.52 us

profile of v4, /device:TPU:0, one launch (start us, length us, event | category | flops | bytes accessed | tf_op | source)
XLA Modules:
  0.0 21.1 jit_solution(16447980609761144047)
XLA Ops:
  0.6 19.9 %score_pair.1 = f32[2,128]{1,0:T(2,128)S(1)} custom-call(s32[1,16]{1,0:T(1,128)} %bits_ref.1, s32[128]{0:T(128)} %labels_ref.1, bf16[16,16384]{1,0:T(8,128)(2,1)} %left_ref.1, bf16[1,2,8,128,128]{4,3,2,1,0:T(8,128)(2,1)} %tens_ref.1), custom_call_target="tpu_custom_call" | custom-call | tf_op jit(solution)/shard_map/score_pair/pallas_call | solution.py:424
  20.5 0.5 %fusion = (f32[1,16]{1,0:T(1,128)}, f32[1,16]{1,0:T(1,128)}) fusion(f32[2,128]{1,0:T(2,128)S(1)} %score_pair.1), kind=kLoop, calls=%fused_computation | loop fusion | bytes 256 | tf_op jit(solution)/shard_map/slice | solution.py:459

commit v5 on v4

--- a/solution.py
+++ b/solution.py
@@ -184,42 +184,59 @@
     bits_v[...] = jnp.zeros_like(bits_v)
     bits_copy.wait()
     bits_v[0:1, 0:rows] = bits_i[...].astype(jnp.float32)
+    pl.semaphore_wait(barrier, ranks)
+
+    pieces0 = [(h, min(2, half - h)) for h in range(0, half, 2)]
+    pieces1 = [(j, min(2, half + 1 - j)) for j in range(0, half + 1, 2)]
+
+    def tens_to_one(i):
+        first, many = pieces0[i]
+        return pltpu.make_async_remote_copy(
+            src_ref=tens_ref.at[0, :, pl.ds(half + first, many)],
+            dst_ref=t0.at[:, pl.ds(first, many)],
+            send_sem=t0_send.at[i],
+            recv_sem=t0_recv.at[i],
+            device_id=(1, blk),
+            device_id_type=MESH,
+        )
+
+    def tens_to_zero(i):
+        first, many = pieces1[i]
+        return pltpu.make_async_remote_copy(
+            src_ref=tens_ref.at[0, :, pl.ds(first, many)],
+            dst_ref=t1.at[:, pl.ds(first, many)],
+            send_sem=t1_send.at[i],
+            recv_sem=t1_recv.at[i],
+            device_id=(0, blk),
+            device_id_type=MESH,
+        )
+
+    def send_piece(i):
+        if i < len(pieces0):
+
+            @pl.when(sect == 0)
+            def _():
+                tens_to_one(i).start()
+
+        @pl.when(sect == 1)
+        def _():
+            tens_to_zero(i).start()
+
+    tens_back = pltpu.make_async_remote_copy(
+        src_ref=tens_ref.at[0, :, pl.ds(0, 1)],
+        dst_ref=t1.at[:, pl.ds(half, 1)],
+        send_sem=t1_send.at[half + 1],
+        recv_sem=t1_recv.at[half + 1],
+        device_id=(1, lax.rem(blk + ranks - 1, ranks)),
+        device_id_type=MESH,
+    )
+
+    send_piece(0)
     inv_copy.wait()
     for b in range(ranks):
         for h in range(half):
             where = inv_s[0, group * b + half * sect + h]
             ordered[b, :, h * block : (h + 1) * block] = left_b[where]
-
-    pl.semaphore_wait(barrier, ranks)
-
-    def tens_to_one(h):
-        return pltpu.make_async_remote_copy(
-            src_ref=tens_ref.at[0, :, pl.ds(half + h, 1)],
-            dst_ref=t0.at[:, pl.ds(h, 1)],
-            send_sem=t0_send.at[h],
-            recv_sem=t0_recv.at[h],
-            device_id=(1, blk),
-            device_id_type=MESH,
-        )
-
-    def tens_to_zero(j):
-        return pltpu.make_async_remote_copy(
-            src_ref=tens_ref.at[0, :, pl.ds(j, 1)],
-            dst_ref=t1.at[:, pl.ds(j, 1)],
-            send_sem=t1_send.at[j],
-            recv_sem=t1_recv.at[j],
-            device_id=(0, blk),
-            device_id_type=MESH,
-        )
-
-    tens_back = pltpu.make_async_remote_copy(
-        src_ref=tens_ref.at[0, :, pl.ds(0, 1)],
-        dst_ref=t1.at[:, pl.ds(half, 1)],
-        send_sem=t1_send.at[half + 1],
-        recv_sem=t1_recv.at[half],
-        device_id=(1, lax.rem(blk + ranks - 1, ranks)),
-        device_id_type=MESH,
-    )
 
     mine = pl.ds(pl.multiple_of(blk * rows, rows), rows)
 
@@ -236,19 +253,11 @@
 
     for i, k in enumerate(far_first):
         send_left(k)
-        if i % 2 == 1 and i // 2 < half:
-
-            @pl.when(sect == 0)
-            def _():
-                tens_to_one(i // 2).start()
-
-            @pl.when(sect == 1)
-            def _():
-                tens_to_zero(i // 2).start()
+        if i % 3 == 2 and 0 < i // 3 + 1 < len(pieces1):
+            send_piece(i // 3 + 1)
 
     @pl.when(sect == 1)
     def _():
-        tens_to_zero(half).start()
         tens_back.start()
 
     state[mine, :] = ordered[blk]
@@ -264,9 +273,11 @@
     sum_raised = jnp.zeros((samples, block), jnp.float32)
     for h in range(half):
 
-        @pl.when(sect == 1)
-        def _():
-            tens_to_one(h).wait_recv()
+        if any(first == h for first, _ in pieces0):
+
+            @pl.when(sect == 1)
+            def _():
+                tens_to_one(h // 2).wait_recv()
 
         both = jnp.concatenate([t0[0, h], t0[1, h]], axis=1)
         image = jnp.dot(
@@ -326,13 +337,17 @@
 
     sums = [[jnp.zeros((samples, block), jnp.float32) for _ in range(2)] for _ in range(2)]
     for j in range(half + 1):
-        if j == half:
-            tens_to_zero(j).wait_recv()
-        else:
+        if any(first == j for first, _ in pieces1):
 
             @pl.when(sect == 0)
             def _():
-                tens_to_zero(j).wait_recv()
+                tens_to_zero(j // 2).wait_recv()
+
+        if j == half:
+
+            @pl.when(sect == 1)
+            def _():
+                tens_back.wait_recv()
 
         both = jnp.concatenate([t1[0, j], t1[1, j]], axis=1)
         twice = jnp.concatenate([both, both], axis=0)
@@ -402,13 +417,13 @@
 
     @pl.when(sect == 0)
     def _():
-        for h in range(half):
-            tens_to_one(h).wait_send()
+        for i in range(len(pieces0)):
+            tens_to_one(i).wait_send()
 
     @pl.when(sect == 1)
     def _():
-        for j in range(half + 1):
-            tens_to_zero(j).wait_send()
+        for i in range(len(pieces1)):
+            tens_to_zero(i).wait_send()
         tens_back.wait_send()
 
 
@@ -447,7 +462,7 @@
             dma((half,)),
             dma((half,)),
             dma((half + 2,)),
-            dma((half + 1,)),
+            dma((half + 2,)),
             dma((2,)),
             dma((2,)),
         ],

time: 21.2 us -> 21 us (level)
  Pallas kernels: 19.9 us -> 19.6 us
    pallas_call x1, Pallas kernels: 19.9 us -> 19.6 us  [body_pair(): pl.pallas_call(functools.partial(pair_kernel, ranks), out_shape=pltpu.VME...]
where the time goes in v5:
time: 21 us; the launch traced here: 20.8 us
  Pallas kernels  19.6 us (93%)
  between operations  0.64 us (3%)
  local copies, waits for them, and re-layouts  0.52 us (2%)
    pallas_call x1, Pallas kernels, body_pair(): pl.pallas_call(functools.partial(pair_kernel, ranks), out_shape=pltpu.VME...  19.6 us
    slice x1, local copies, waits for them, and re-layouts, body_pair(): return (scored[0:1, :rows], scored[1:2, :rows])  0.52 us

profile of v5, /device:TPU:0, one launch (start us, length us, event | category | flops | bytes accessed | tf_op | source)
XLA Modules:
  0.0 20.8 jit_solution(6894699946529019784)
XLA Ops:
  0.6 19.6 %score_pair.1 = f32[2,128]{1,0:T(2,128)S(1)} custom-call(s32[1,16]{1,0:T(1,128)} %bits_ref.1, s32[128]{0:T(128)} %labels_ref.1, bf16[16,16384]{1,0:T(8,128)(2,1)} %left_ref.1, bf16[1,2,8,128,128]{4,3,2,1,0:T(8,128)(2,1)} %tens_ref.1), custom_call_target="tpu_custom_call" | custom-call | tf_op jit(solution)/shard_map/score_pair/pallas_call | solution.py:439
  20.3 0.5 %fusion = (f32[1,16]{1,0:T(1,128)}, f32[1,16]{1,0:T(1,128)}) fusion(f32[2,128]{1,0:T(2,128)S(1)} %score_pair.1), kind=kLoop, calls=%fused_computation | loop fusion | bytes 256 | tf_op jit(solution)/shard_map/slice | solution.py:474

commit v6 on v5

--- a/solution.py
+++ b/solution.py
@@ -114,6 +114,7 @@
     ordered,
     state,
     images,
+    sums,
     t0,
     t1,
     part0,
@@ -179,8 +180,14 @@
     inv_copy = pltpu.make_async_copy(inv_v, inv_s, local_sem.at[2])
     inv_copy.start()
     left_copy.wait()
-    for i in range(count_blocks):
-        left_b[i] = left_v[:, i * block : (i + 1) * block]
+
+    def stage(step, carry):
+        for u in range(8):
+            i = step * 8 + u
+            left_b[i] = left_v[:, pl.ds(pl.multiple_of(i * block, block), block)]
+        return carry
+
+    lax.fori_loop(0, count_blocks // 8, stage, 0)
     bits_v[...] = jnp.zeros_like(bits_v)
     bits_copy.wait()
     bits_v[0:1, 0:rows] = bits_i[...].astype(jnp.float32)
@@ -233,10 +240,14 @@
 
     send_piece(0)
     inv_copy.wait()
-    for b in range(ranks):
+
+    def order(b, carry):
         for h in range(half):
             where = inv_s[0, group * b + half * sect + h]
             ordered[b, :, h * block : (h + 1) * block] = left_b[where]
+        return carry
+
+    lax.fori_loop(0, ranks, order, 0)
 
     mine = pl.ds(pl.multiple_of(blk * rows, rows), rows)
 
@@ -269,26 +280,30 @@
     def _():
         own_t0.wait()
 
-    sum_stay = jnp.zeros((samples, block), jnp.float32)
-    sum_raised = jnp.zeros((samples, block), jnp.float32)
-    for h in range(half):
-
-        if any(first == h for first, _ in pieces0):
-
-            @pl.when(sect == 1)
+    sums[...] = jnp.zeros_like(sums)
+
+    def site_zero(h, carry):
+        for i, (first, _) in enumerate(pieces0):
+
+            @pl.when((sect == 1) & (h == first))
             def _():
-                tens_to_one(h // 2).wait_recv()
+                tens_to_one(i).wait_recv()
 
         both = jnp.concatenate([t0[0, h], t0[1, h]], axis=1)
         image = jnp.dot(
-            state[:, h * block : (h + 1) * block], both, preferred_element_type=jnp.float32
+            state[:, pl.ds(pl.multiple_of(h * block, block), block)],
+            both,
+            preferred_element_type=jnp.float32,
         )
         images[h] = image
         stay, raised = image[:, :block], image[:, block:]
-        sum_stay += stay * stay
-        sum_raised += raised * raised
-    norm_stay = jnp.sum(sum_stay, axis=1, keepdims=True)
-    norm_raised = jnp.sum(sum_raised, axis=1, keepdims=True)
+        sums[0] += stay * stay
+        sums[1] += raised * raised
+        return carry
+
+    lax.fori_loop(0, half, site_zero, 0)
+    norm_stay = jnp.sum(sums[0], axis=1, keepdims=True)
+    norm_raised = jnp.sum(sums[1], axis=1, keepdims=True)
 
     lane = lax.broadcasted_iota(jnp.int32, (samples, block), 1)
     row = lax.broadcasted_iota(jnp.int32, (samples, block), 0)
@@ -335,42 +350,34 @@
     def _():
         own_t1.wait()
 
-    sums = [[jnp.zeros((samples, block), jnp.float32) for _ in range(2)] for _ in range(2)]
-    for j in range(half + 1):
-        if any(first == j for first, _ in pieces1):
-
-            @pl.when(sect == 0)
+    def site_one(h, carry):
+        for i, (first, _) in enumerate(pieces1):
+
+            @pl.when((sect == 0) & (h == max(first - 1, 0)))
             def _():
-                tens_to_zero(j // 2).wait_recv()
-
-        if j == half:
-
-            @pl.when(sect == 1)
-            def _():
-                tens_back.wait_recv()
-
-        both = jnp.concatenate([t1[0, j], t1[1, j]], axis=1)
-        twice = jnp.concatenate([both, both], axis=0)
-        firsts = [first for first in range(2) if 0 <= j - first < half]
-        values = [
-            images[j - first, :, first * block : (first + 1) * block] * scales[first]
-            for first in firsts
-        ]
-        image = jnp.dot(
-            jnp.concatenate([halves(value) for value in values], axis=0),
-            twice,
-            preferred_element_type=jnp.float32,
-        )
-        for i, first in enumerate(firsts):
+                tens_to_zero(i).wait_recv()
+
+        @pl.when((sect == 1) & (h == half - 1))
+        def _():
+            tens_back.wait_recv()
+
+        for first in range(2):
+            both = jnp.concatenate([t1[0, h + first], t1[1, h + first]], axis=1)
+            value = images[h, :, first * block : (first + 1) * block] * scales[first]
+            image = jnp.dot(
+                halves(value),
+                jnp.concatenate([both, both], axis=0),
+                preferred_element_type=jnp.float32,
+            )
             for second in range(2):
-                piece = image[
-                    i * samples : (i + 1) * samples, second * block : (second + 1) * block
-                ]
-                sums[first][second] += piece * piece
+                piece = image[:, second * block : (second + 1) * block]
+                sums[2 + 2 * second + first] += piece * piece
+        return carry
+
+    lax.fori_loop(0, half, site_one, 0)
     columns = [norm_stay, norm_raised]
-    for second in range(2):
-        for first in range(2):
-            columns.append(jnp.sum(sums[first][second], axis=1, keepdims=True))
+    for v in range(2, 6):
+        columns.append(jnp.sum(sums[v], axis=1, keepdims=True))
     fill(part1, columns)
     own_bits = pltpu.roll(bits_v[...], 6 * rows, 1)[0:1]
     part1[blk] = part1[blk] + jnp.where(sect == 0, own_bits, 0.0)
@@ -451,6 +458,7 @@
             pltpu.VMEM((ranks, rows, half * block), jnp.bfloat16),
             pltpu.VMEM((ranks * rows, half * block), jnp.bfloat16),
             pltpu.VMEM((half, ranks * rows, 2 * block), jnp.float32),
+            pltpu.VMEM((6, ranks * rows, block), jnp.float32),
             pltpu.VMEM((2, half, block, block), jnp.bfloat16),
             pltpu.VMEM((2, half + 1, block, block), jnp.bfloat16),
             pltpu.VMEM((ranks, 1, block), jnp.float32),

time: 21 us -> 21.4 us (1.019)
  Pallas kernels: 19.6 us -> 20.1 us
    pallas_call x1, Pallas kernels: 19.6 us -> 20.1 us  [body_pair(): pl.pallas_call(functools.partial(pair_kernel, ranks), out_shape=pltpu.VME...]
where the time goes in v6:
time: 21.4 us; the launch traced here: 21.3 us
  Pallas kernels  20.1 us (94%)
  between operations  0.64 us (3%)
  local copies, waits for them, and re-layouts  0.52 us (2%)
    pallas_call x1, Pallas kernels, body_pair(): pl.pallas_call(functools.partial(pair_kernel, ranks), out_shape=pltpu.VME...  20.1 us
    slice x1, local copies, waits for them, and re-layouts, body_pair(): return (scored[0:1, :rows], scored[1:2, :rows])  0.52 us

profile of v6, /device:TPU:0, one launch (start us, length us, event | category | flops | bytes accessed | tf_op | source)
XLA Modules:
  0.0 21.3 jit_solution(16636183325691432385)
XLA Ops:
  0.6 20.1 %score_pair.1 = f32[2,128]{1,0:T(2,128)S(1)} custom-call(s32[1,16]{1,0:T(1,128)} %bits_ref.1, s32[128]{0:T(128)} %labels_ref.1, bf16[16,16384]{1,0:T(8,128)(2,1)} %left_ref.1, bf16[1,2,8,128,128]{4,3,2,1,0:T(8,128)(2,1)} %tens_ref.1), custom_call_target="tpu_custom_call" | custom-call | tf_op jit(solution)/shard_map/score_pair/pallas_call | solution.py:446
  20.8 0.5 %fusion = (f32[1,16]{1,0:T(1,128)}, f32[1,16]{1,0:T(1,128)}) fusion(f32[2,128]{1,0:T(2,128)S(1)} %score_pair.1), kind=kLoop, calls=%fused_computation | loop fusion | bytes 256 | tf_op jit(solution)/shard_map/slice | solution.py:482
